TPU v7x, 32 devices: a whole 2x2x4 slice. The times are simulated.
32 devices in a mesh: chan: 4 (over y, core), tile: 8 (over z, x).
Axes of the slice: x: 2, y: 2, z: 4, core: 2. Of those that a mesh axis runs over, the one named last changes fastest.
Arguments:
- intensity: bfloat16 [256, 256, 512], P('chan', 'tile'), may hold values from -12 to 12
- block_pick: int32 [8, 4, 4], P('tile', 'chan'), may hold values from 0 to 7, as said below
- owner_tile: int32 [8, 4, 4], P('tile', 'chan'), may hold values from 0 to 7, as said below
- source_index: int32 [8, 4, 4], P('tile', 'chan'), may hold values from 0 to 15
- mask_low: int32 [8, 4, 4, 1024], P('tile', 'chan'), may hold values from 0 to 63
- mask_high: int32 [8, 4, 4, 1024], P('tile', 'chan'), may hold values from 64 to 128
Outputs:
- moment_maps: float32 [8, 4, 8, 2, 1024], P('tile', 'chan')
- spectra: float32 [8, 4, 16, 256], P('tile', 'chan')
- smoothed: bfloat16 [256, 256, 512], P(None, 'tile', 'chan')
Inputs may be any that keep to these rules, and one draw needn't show every extreme that they name: `block_pick`: the 4 block numbers of one device are distinct. `owner_tile`: among the 4 sends of one device no owner appears more than 2 times; in every chan index some owner receives exactly 2 blocks from every device of that chan index.
All inputs are finite; a program needn't handle non-finite values.
Results may differ from a plain program's by a relative error of at most 0.0021.
Values may be sent and summed in bfloat16 or wider, within the bound.
A program may use at most 128 MiB of HBM per device.

v0:
```python
import jax
import jax.numpy as jnp
from jax import lax
from jax.sharding import PartitionSpec as P

BCH = 128
BPIX = 32
RADIUS = 2
CAP = 2
SRC_DEV = 16


SIGMA = 1.5


def with_halo(block, sides, width):
    for axis, dim in sides:
        count = lax.axis_size(axis)
        forward = [(i, i + 1) for i in range(count - 1)]
        backward = [(target, source) for source, target in forward]
        low = lax.ppermute(
            lax.slice_in_dim(block, block.shape[dim] - width, None, axis=dim), axis, forward
        )
        high = lax.ppermute(lax.slice_in_dim(block, 0, width, axis=dim), axis, backward)
        block = jnp.concatenate([low, block, high], axis=dim)
    return block


def gauss_weights():
    offsets = jnp.arange(-RADIUS, RADIUS + 1).astype(jnp.float32)
    raw_weights = jnp.exp(-offsets * offsets / (2.0 * SIGMA * SIGMA))
    return raw_weights / jnp.sum(raw_weights)


def smooth_tiles(framed):
    chan_total = framed.shape[0]
    rows_inner = framed.shape[1] - 2 * RADIUS
    cols_inner = framed.shape[2] - 2 * RADIUS
    chan_blocks = chan_total // BCH
    weights = gauss_weights()

    def smooth_block(block_index):
        first_chan = block_index * BCH
        middle = lax.dynamic_slice_in_dim(framed, first_chan, BCH, 0).astype(jnp.float32)
        before = lax.dynamic_slice_in_dim(framed, jnp.maximum(first_chan - 1, 0), 1, 0).astype(
            jnp.float32
        )
        before = before * (block_index > 0).astype(jnp.float32)
        after = lax.dynamic_slice_in_dim(
            framed, jnp.minimum(first_chan + BCH, chan_total - 1), 1, 0
        ).astype(jnp.float32)
        after = after * (block_index < chan_blocks - 1).astype(jnp.float32)
        lower = jnp.concatenate([before, middle[:-1]], axis=0)
        upper = jnp.concatenate([middle[1:], after], axis=0)
        hanning = 0.5 * middle + 0.25 * (lower + upper)
        row_pass = sum(
            (
                weights[offset] * hanning[:, offset : offset + rows_inner, :]
                for offset in range(2 * RADIUS + 1)
            )
        )
        col_pass = sum(
            (
                weights[offset] * row_pass[:, :, offset : offset + cols_inner]
                for offset in range(2 * RADIUS + 1)
            )
        )
        return col_pass.astype(jnp.bfloat16)

    stacked = lax.map(smooth_block, jnp.arange(chan_blocks, dtype=jnp.int32))
    return stacked.reshape(chan_total, rows_inner, cols_inner)


def per_device(intensity, block_pick, owner_tile, source_index, mask_low, mask_high):
    regrouped = lax.all_to_all(intensity, "chan", split_axis=2, concat_axis=0, tiled=True)
    framed = with_halo(regrouped, (("chan", 2), ("tile", 1)), RADIUS)
    tile_cube = smooth_tiles(framed)
    chan_total, rows_inner, cols_inner = tile_cube.shape
    chan_blocks = chan_total // BCH
    block_rows = rows_inner // BPIX
    block_cols = cols_inner // BPIX
    per_chan_block = block_rows * block_cols
    pixel_count = mask_low.shape[-1]
    picks = block_pick.reshape(-1)
    owners = owner_tile.reshape(-1)
    sources = source_index.reshape(-1)
    send_count = picks.shape[0]
    low_rows = mask_low.reshape(send_count, pixel_count)
    high_rows = mask_high.reshape(send_count, pixel_count)
    chan_of = picks // per_chan_block
    positions = jnp.arange(send_count, dtype=jnp.int32)
    earlier = (positions[None, :] < positions[:, None]) & (owners[None, :] == owners[:, None])
    ranking = jnp.sum(earlier.astype(jnp.int32), axis=1)
    slot_of = owners * CAP + ranking
    peer_count = lax.axis_size("tile")
    slot_total = peer_count * CAP
    filled = slot_of[None, :] == jnp.arange(slot_total, dtype=jnp.int32)[:, None]
    occupied = jnp.any(filled, axis=1)
    sender = jnp.sum(jnp.where(filled, positions[None, :], 0), axis=1)
    tags = jnp.stack([jnp.where(occupied, sources[sender], -1), chan_of[sender]], axis=1).reshape(
        peer_count, CAP, 2
    )
    block_total = chan_blocks * per_chan_block
    low_grid = jnp.zeros((block_total, pixel_count), jnp.int32).at[picks].set(low_rows)
    high_grid = jnp.zeros((block_total, pixel_count), jnp.int32).at[picks].set(high_rows)

    def to_tile(grid):
        shaped = grid.reshape(chan_blocks, block_rows, block_cols, BPIX, BPIX).transpose(
            0, 1, 3, 2, 4
        )
        return shaped.reshape(chan_blocks, 1, rows_inner, cols_inner)

    low_tile = to_tile(low_grid)
    high_tile = to_tile(high_grid)
    cube_blocks = tile_cube.reshape(chan_blocks, BCH, rows_inner, cols_inner)
    chan_pos = jnp.arange(BCH, dtype=jnp.int32).reshape(1, BCH, 1, 1)
    inside = (low_tile <= chan_pos) & (chan_pos < high_tile)
    masked = jnp.where(inside, cube_blocks.astype(jnp.float32), 0.0)
    maps_tile = jnp.sum(masked, axis=1)
    spectra_tile = jnp.sum(
        masked.reshape(chan_blocks, BCH, block_rows, BPIX, block_cols, BPIX), axis=(3, 5)
    )
    all_maps = (
        maps_tile.reshape(chan_blocks, block_rows, BPIX, block_cols, BPIX)
        .transpose(0, 1, 3, 2, 4)
        .reshape(block_total, pixel_count)
    )
    all_spectra = spectra_tile.transpose(0, 2, 3, 1).reshape(block_total, BCH)
    slot_picks = picks[sender]
    maps_slots = jnp.where(occupied[:, None], all_maps[slot_picks], 0.0).reshape(
        peer_count, CAP, pixel_count
    )
    spectra_slots = jnp.where(occupied[:, None], all_spectra[slot_picks], 0.0).reshape(
        peer_count, CAP, BCH
    )
    maps_here, spectra_here, tags_here = (
        lax.all_to_all(maps_slots, "tile", split_axis=0, concat_axis=0, tiled=True),
        lax.all_to_all(spectra_slots, "tile", split_axis=0, concat_axis=0, tiled=True),
        lax.all_to_all(tags, "tile", split_axis=0, concat_axis=0, tiled=True),
    )
    moment_maps = maps_here.reshape(1, 1, peer_count, CAP, pixel_count)
    keys_here = (tags_here[..., 0] * chan_blocks + tags_here[..., 1]).reshape(-1)
    selector = (
        keys_here[None, :] == jnp.arange(SRC_DEV * chan_blocks, dtype=jnp.int32)[:, None]
    ).astype(jnp.float32)
    spectra = jnp.dot(
        selector,
        spectra_here.reshape(-1, BCH),
        precision=lax.Precision.HIGHEST,
        preferred_element_type=jnp.float32,
    )
    return (moment_maps, spectra.reshape(1, 1, SRC_DEV, chan_blocks * BCH), tile_cube)


def solution(mesh):
    return jax.shard_map(
        per_device,
        mesh=mesh,
        in_specs=(
            P("chan", "tile", None),
            P("tile", "chan", None),
            P("tile", "chan", None),
            P("tile", "chan", None),
            P("tile", "chan", None, None),
            P("tile", "chan", None, None),
        ),
        out_specs=(
            P("tile", "chan", None, None, None),
            P("tile", "chan", None, None),
            P(None, "tile", "chan"),
        ),
        check_vma=False,
    )
```

profile of v0, /device:TPU:0, one launch (start us, length us, event | category | flops | bytes accessed | tf_op | source)
XLA Modules:
  0.0 183.3 jit_solution(6895373197032733767)
XLA Ops:
  0.6 8.8 %copy.87 = bf16[64,32,512]{0,1,2:T(8,128)(2,1)} copy(bf16[64,32,512]{2,1,0:T(8,128)(2,1)} %param.8) | data formatting | bytes 4194304 | tf_op args[0]
  9.4 5.9 %reshape.268 = bf16[4,2,131072]{2,1,0:T(2,128)(2,1)} reshape(bf16[512,32,64]{2,1,0:T(8,128)(2,1)} %bitcast.84) | data formatting | bytes 4194304
  15.3 4.4 %all-to-all-start = ((bf16[4,2,131072]{2,1,0:T(2,128)(2,1)}), bf16[4,2,131072]{2,1,0:T(2,128)(2,1)S(1)}, u32[]{:S(2)}, u32[]{:S(2)}) async-start(bf16[4,2,131072]{2,1,0:T(2,128)(2,1)} %reshape.268), calls=%async_computation | async-start | bytes 4194304 | tf_op jit(solution)/shard_map/all_to_all | solution.py:75
  22.9 22.5 %all-to-all-done = bf16[4,2,131072]{2,1,0:T(2,128)(2,1)S(1)} async-done(((bf16[4,2,131072]{2,1,0:T(2,128)(2,1)}), bf16[4,2,131072]{2,1,0:T(2,128)(2,1)S(1)}, u32[]{:S(2)}, u32[]{:S(2)}) %all-to-all-start) | async-done | bytes 2097184 | tf_op jit(solution)/shard_map/all_to_all | solution.py:75
  45.4 6.6 %all-to-all-start.2 = ((s32[8,2,2]{1,2,0:T(2,128)}), s32[8,2,2]{1,2,0:T(2,128)S(1)}, u32[]{:S(2)}, u32[]{:S(2)}) async-start(s32[8,2,2]{1,2,0:T(2,128)} %copy.98), calls=%async_computation.2 | async-start | bytes 16384 | tf_op jit(solution)/shard_map/all_to_all | solution.py:139
  52.0 4.0 %reshape.269 = bf16[512,32,64]{2,1,0:T(8,128)(2,1)} reshape(bf16[4,2,131072]{2,1,0:T(2,128)(2,1)S(1)} %all-to-all-done) | data formatting | bytes 4194304
  56.0 6.8 %copy.102 = bf16[64,32,4,128]{3,2,1,0:T(4,128)(2,1)} copy(bf16[64,32,4,128]{0,1,3,2:T(8,128)(2,1)} %bitcast.83) | data formatting | bytes 4194304 | tf_op jit(solution)/shard_map/all_to_all | solution.py:75
  62.8 1.9 %copy.89 = bf16[4,64,32,128]{3,2,1,0:T(8,128)(2,1)S(1)} copy(bf16[4,64,32,128]{3,0,2,1:T(4,128)(2,1)} %bitcast.85) | data formatting | bytes 4194304 | tf_op jit(solution)/shard_map/all_to_all | solution.py:75
  64.8 3.0 %fusion.34 = (bf16[256,32,2]{2,1,0:T(8,128)(2,1)}, bf16[256,32,2]{2,1,0:T(8,128)(2,1)}) fusion(bf16[256,32,128]{2,1,0:T(8,128)(2,1)S(1)} %bitcast.81), kind=kLoop, calls=%fused_computation.85 | loop fusion | bytes 131072 | tf_op jit(solution)/shard_map/slice | solution.py:22
  67.7 3.3 %copy.90 = bf16[256,32,2]{0,1,2:T(8,128)(2,1)S(1)} copy(bf16[256,32,2]{2,1,0:T(8,128)(2,1)} %get-tuple-element.92) | data formatting | bytes 65536 | tf_op jit(solution)/shard_map/slice | solution.py:22
  72.3 3.3 %copy.91 = bf16[256,32,2]{0,1,2:T(8,128)(2,1)S(1)} copy(bf16[256,32,2]{2,1,0:T(8,128)(2,1)} %get-tuple-element.93) | data formatting | bytes 65536 | tf_op jit(solution)/shard_map/slice | solution.py:24
  75.6 1.5 collective-permute-start.1
  77.7 4.2 %copy.92 = bf16[256,32,2]{2,1,0:T(8,128)(2,1)} copy(bf16[256,32,2]{0,1,2:T(8,128)(2,1)S(1)} %collective-permute-done) | data formatting | bytes 65536 | tf_op jit(solution)/shard_map/ppermute | solution.py:21
  81.9 4.2 %copy.93 = bf16[256,32,2]{2,1,0:T(8,128)(2,1)} copy(bf16[256,32,2]{0,1,2:T(8,128)(2,1)S(1)} %collective-permute-done.1) | data formatting | bytes 65536 | tf_op jit(solution)/shard_map/ppermute | solution.py:24
  86.1 4.3 %pad_maximum_fusion = bf16[256,32,132]{2,1,0:T(8,128)(2,1)S(1)} fusion(bf16[256,32,2]{2,1,0:T(8,128)(2,1)} %copy.93, bf16[256,32,128]{2,1,0:T(8,128)(2,1)S(1)} %bitcast.82, bf16[256,32,2]{2,1,0:T(8,128)(2,1)} %copy.92), kind=kLoop, calls=%fused_computation.33 | loop fusion | flops 6488064 | bytes 4325376 | tf_op jit(solution)/shard_map/concatenate | solution.py:25
  90.4 1.9 %copy-done.5 = bf16[256,32,132]{2,1,0:T(8,128)(2,1)} copy-done((bf16[256,32,132]{2,1,0:T(8,128)(2,1)}, bf16[256,32,132]{2,1,0:T(8,128)(2,1)S(1)}, u32[]{:S(2)}) %copy-start.5) | copy-done | bytes 2162712
  92.7 3.9 %collective-permute-start.2 = (bf16[256,2,132]{2,1,0:T(2,128)(2,1)S(1)}, bf16[256,2,132]{2,1,0:T(2,128)(2,1)S(1)}, u32[]{:S(2)}, u32[]{:S(2)}) collective-permute-start(bf16[256,2,132]{2,1,0:T(2,128)(2,1)S(1)} %get-tuple-element.90), channel_id=1, source_target_pairs={{0,1},{1,2},{2,3},{3,4},{4,5},{5,6},{6,7},{8,9},{9,10},{10,11},{11... | collective-permute-start | bytes 405512 | tf_op jit(solution)/shard_map/ppermute | solution.py:21
  100.9 7.6 %copy.95 = bf16[256,32,132]{0,2,1:T(8,128)(2,1)} copy(bf16[256,32,132]{2,1,0:T(8,128)(2,1)} %copy-done.5) | data formatting | bytes 4325376 | tf_op jit(solution)/shard_map/concatenate | solution.py:25
  108.9 2.0 %pad_maximum_fusion.1 = bf16[256,36,132]{0,2,1:T(8,128)(2,1)S(1)} fusion(bf16[256,2,132]{0,2,1:T(8,128)(2,1)S(1)} %copy.96, bf16[256,32,132]{0,2,1:T(8,128)(2,1)} %copy.95, bf16[256,2,132]{0,2,1:T(8,128)(2,1)S(1)} %copy.94), kind=kLoop, calls=%fused_computation.40 | loop fusion | flops 2433024 | bytes 4866048 | tf_op jit(solution)/shard_map/concatenate | solution.py:25
  110.8 38.9 %while.12 = (s32[]{:T(128)}, bf16[2,128,32,128]{1,3,2,0:T(8,128)(2,1)}, f32[5]{0:T(128)S(1)}, s32[2]{0:T(128)S(1)}, bf16[256,36,132]{0,2,1:T(8,128)(2,1)S(1)}, /...) while((s32[]{:T(128)}, ...), condition=%wide.region_6.7_spmd, body=%wide.region_5.6_spmd.sunk | while | flops 14994001 | bytes 46544248 | solution.py:70
  113.4 3.0 %convert_multiply_fusion.3 = (f32[1,36,132]{0,2,1:T(8,128)}, f32[1,36,132]{0,2,1:T(8,128)}) fusion(f32[]{:T(128)} %bitcast.72, bf16[256,36,132]{0,2,1:T(8,128)(2,1)S(1)} %get-tuple-element.175, s32[]{:T(128)S(6)} %select_n.117, f32[]{:T(128)} %bitcast.73, s32[]{:T(128)S(6)} %max.7), kind=kLoop, calls=%fused_computation.10.clone.1 | loop fusion | flops 19008 | bytes 57040 | tf_op jit(solution)/shard_map/while/body/eval_jaxpr/mul | solution.py:52
  119.0 1.4 fusion.41
  121.1 3.8 %fusion.43 = f32[128,32,132]{0,2,1:T(8,128)S(1)} fusion(f32[128,36,132]{0,2,1:T(8,128)S(1)} %fusion.41, f32[]{:T(128)} %bitcast.74, f32[]{:T(128)} %bitcast.75, f32[]{:T(128)} %bitcast.76, f32[]{:T(128)} %bitcast.77, f32[]{:T(128)} %bitcast.78), kind=kLoop, calls=%fused_computation.13.clone.1 | loop fusion | flops 4866048 | bytes 12976148 | tf_op jit(solution)/shard_map/while/body/eval_jaxpr/add | solution.py:56
  124.9 5.4 %bitcast_dynamic-update-slice_fusion.2 = bf16[2,128,32,128]{1,3,2,0:T(8,128)(2,1)} fusion(bf16[2,128,32,128]{1,3,2,0:T(8,128)(2,1)} %get-tuple-element.158, s32[]{:T(128)} %get-tuple-element.157, f32[128,32,132]{0,2,1:T(8,128)S(1)} %fusion.43, f32[]{:T(128)} %bitcast.74, f32[]{:T(128)} %bitcast.75, f32[]{:T(128)} %bitcast.76, f32[]{:T(128)} %bitcast.77, ...), kind=kLoop, calls=%fused_computation.32.clone.1 | loop fusion | flops 5242880 | bytes 11537408 | tf_op jit(solution)/shard_map/while/body/jit(dynamic_update_index_in_dim)/dynamic_update_slice | solution.py:70
  132.8 3.0 %convert_multiply_fusion.3 = (f32[1,36,132]{0,2,1:T(8,128)}, f32[1,36,132]{0,2,1:T(8,128)}) fusion(f32[]{:T(128)} %bitcast.72, bf16[256,36,132]{0,2,1:T(8,128)(2,1)S(1)} %get-tuple-element.175, s32[]{:T(128)S(6)} %select_n.117, f32[]{:T(128)} %bitcast.73, s32[]{:T(128)S(6)} %max.7), kind=kLoop, calls=%fused_computation.10.clone.1 | loop fusion | flops 19008 | bytes 57040 | tf_op jit(solution)/shard_map/while/body/eval_jaxpr/mul | solution.py:52
  140.5 3.8 %fusion.43 = f32[128,32,132]{0,2,1:T(8,128)S(1)} fusion(f32[128,36,132]{0,2,1:T(8,128)S(1)} %fusion.41, f32[]{:T(128)} %bitcast.74, f32[]{:T(128)} %bitcast.75, f32[]{:T(128)} %bitcast.76, f32[]{:T(128)} %bitcast.77, f32[]{:T(128)} %bitcast.78), kind=kLoop, calls=%fused_computation.13.clone.1 | loop fusion | flops 4866048 | bytes 12976148 | tf_op jit(solution)/shard_map/while/body/eval_jaxpr/add | solution.py:56
  144.3 5.4 %bitcast_dynamic-update-slice_fusion.2 = bf16[2,128,32,128]{1,3,2,0:T(8,128)(2,1)} fusion(bf16[2,128,32,128]{1,3,2,0:T(8,128)(2,1)} %get-tuple-element.158, s32[]{:T(128)} %get-tuple-element.157, f32[128,32,132]{0,2,1:T(8,128)S(1)} %fusion.43, f32[]{:T(128)} %bitcast.74, f32[]{:T(128)} %bitcast.75, f32[]{:T(128)} %bitcast.76, f32[]{:T(128)} %bitcast.77, ...), kind=kLoop, calls=%fused_computation.32.clone.1 | loop fusion | flops 5242880 | bytes 11537408 | tf_op jit(solution)/shard_map/while/body/jit(dynamic_update_index_in_dim)/dynamic_update_slice | solution.py:70
  149.7 6.1 %fusion.11 = (f32[2,128,128]{1,2,0:T(8,128)S(1)}, f32[2,32,128]{2,1,0:T(8,128)S(1)}) fusion(bf16[2,128,32,128]{1,3,2,0:T(8,128)(2,1)} %get-tuple-element.68, s32[2,32,128]{2,1,0:T(8,128)S(1)} %lt.89, s32[2,32,128]{2,1,0:T(8,128)S(1)} %le.17), kind=kLoop, calls=%fused_computation.35 | loop fusion | flops 7299072 | bytes 2326528 | tf_op jit(solution)/shard_map/reduce_sum | solution.py:120
  157.1 6.6 %all-to-all-start.3 = ((f32[8,2,128]{2,1,0:T(2,128)}), f32[8,2,128]{2,1,0:T(2,128)S(1)}, u32[]{:S(2)}, u32[]{:S(2)}) async-start(f32[8,2,128]{2,1,0:T(2,128)} %broadcast_select_fusion.1), calls=%async_computation.3 | async-start | bytes 16384 | tf_op jit(solution)/shard_map/all_to_all | solution.py:138
  165.3 4.5 %copy.101 = bf16[2,128,32,128]{3,2,1,0:T(8,128)(2,1)} copy(bf16[2,128,32,128]{1,3,2,0:T(8,128)(2,1)} %get-tuple-element.68) | data formatting | bytes 4194304 | tf_op jit(solution)/shard_map/while | solution.py:70
  170.2 5.6 %all-to-all-start.1 = ((f32[8,2,1024]{2,1,0:T(2,128)}), f32[8,2,1024]{2,1,0:T(2,128)S(1)}, u32[]{:S(2)}, u32[]{:S(2)}) async-start(f32[8,2,1024]{2,1,0:T(2,128)} %broadcast_select_fusion), calls=%async_computation.1 | async-start | bytes 131072 | tf_op jit(solution)/shard_map/all_to_all | solution.py:137
  176.6 6.2 %all-to-all-done.1 = f32[8,2,1024]{2,1,0:T(2,128)S(1)} async-done(((f32[8,2,1024]{2,1,0:T(2,128)}), f32[8,2,1024]{2,1,0:T(2,128)S(1)}, u32[]{:S(2)}, u32[]{:S(2)}) %all-to-all-start.1) | async-done | bytes 65568 | tf_op jit(solution)/shard_map/all_to_all | solution.py:137
  (84 shorter events, 23.8 us)
Async XLA Ops:
  0.6 98.1 %copy-start = (s32[1,1,4,1024]{3,2,1,0:T(4,128)S(1)}, s32[1,1,4,1024]{3,2,1,0:T(4,128)}, u32[]{:S(2)}) copy-start(s32[1,1,4,1024]{3,2,1,0:T(4,128)} %param.12) | copy-start | bytes 49156
  15.3 4.4 %copy-start.7 = (s32[1,1,4]{2,1,0:T(1,128)S(1)}, s32[1,1,4]{2,1,0:T(1,128)}, u32[]{:S(2)}) copy-start(s32[1,1,4]{2,1,0:T(1,128)} %param.10) | copy-start | bytes 52
  15.3 4.7 %copy-start.2 = (s32[1,1,4]{2,1,0:T(1,128)S(1)}, s32[1,1,4]{2,1,0:T(1,128)}, u32[]{:S(2)}) copy-start(s32[1,1,4]{2,1,0:T(1,128)} %param.9) | copy-start | bytes 52
  15.3 5.3 %copy-start.1 = (s32[1,1,4]{2,1,0:T(1,128)S(1)}, s32[1,1,4]{2,1,0:T(1,128)}, u32[]{:S(2)}) copy-start(s32[1,1,4]{2,1,0:T(1,128)} %param.11) | copy-start | bytes 52
  15.3 30.1 %all-to-all-start = ((bf16[4,2,131072]{2,1,0:T(2,128)(2,1)}), bf16[4,2,131072]{2,1,0:T(2,128)(2,1)S(1)}, u32[]{:S(2)}, u32[]{:S(2)}) async-start(bf16[4,2,131072]{2,1,0:T(2,128)(2,1)} %reshape.268), calls=%async_computation | async-start | bytes 4194304 | tf_op jit(solution)/shard_map/all_to_all | solution.py:75
  45.4 55.4 %all-to-all-start.2 = ((s32[8,2,2]{1,2,0:T(2,128)}), s32[8,2,2]{1,2,0:T(2,128)S(1)}, u32[]{:S(2)}, u32[]{:S(2)}) async-start(s32[8,2,2]{1,2,0:T(2,128)} %copy.98), calls=%async_computation.2 | async-start | bytes 16384 | tf_op jit(solution)/shard_map/all_to_all | solution.py:139
  71.0 6.7 %collective-permute-start = (bf16[256,32,2]{0,1,2:T(8,128)(2,1)S(1)}, bf16[256,32,2]{0,1,2:T(8,128)(2,1)S(1)}, u32[]{:S(2)}, u32[]{:S(2)}) collective-permute-start(bf16[256,32,2]{0,1,2:T(8,128)(2,1)S(1)} %copy.90), channel_id=1, source_target_pairs={{0,8},{8,16},{16,24},{1,9},{9,17},{17,25},{2,10},{10,18},{18,26},{... | collective-permute-start | bytes 98312 | tf_op jit(solution)/shard_map/ppermute | solution.py:21
  75.6 6.3 %collective-permute-start.1 = (bf16[256,32,2]{0,1,2:T(8,128)(2,1)S(1)}, bf16[256,32,2]{0,1,2:T(8,128)(2,1)S(1)}, u32[]{:S(2)}, u32[]{:S(2)}) collective-permute-start(bf16[256,32,2]{0,1,2:T(8,128)(2,1)S(1)} %copy.91), channel_id=1, source_target_pairs={{8,0},{16,8},{24,16},{9,1},{17,9},{25,17},{10,2},{18,10},{26,18},{... | collective-permute-start | bytes 98312 | tf_op jit(solution)/shard_map/ppermute | solution.py:24
  86.1 13.6 %copy-start.6 = (s32[1,1,4,1024]{3,2,1,0:T(4,128)S(1)}, s32[1,1,4,1024]{3,2,1,0:T(4,128)}, u32[]{:S(2)}) copy-start(s32[1,1,4,1024]{3,2,1,0:T(4,128)} %param.13) | copy-start | bytes 49156
  90.3 1.9 %copy-start.5 = (bf16[256,32,132]{2,1,0:T(8,128)(2,1)}, bf16[256,32,132]{2,1,0:T(8,128)(2,1)S(1)}, u32[]{:S(2)}) copy-start(bf16[256,32,132]{2,1,0:T(8,128)(2,1)S(1)} %pad_maximum_fusion) | copy-start | bytes 6488068
  92.7 15.8 %collective-permute-start.2 = (bf16[256,2,132]{2,1,0:T(2,128)(2,1)S(1)}, bf16[256,2,132]{2,1,0:T(2,128)(2,1)S(1)}, u32[]{:S(2)}, u32[]{:S(2)}) collective-permute-start(bf16[256,2,132]{2,1,0:T(2,128)(2,1)S(1)} %get-tuple-element.90), channel_id=1, source_target_pairs={{0,1},{1,2},{2,3},{3,4},{4,5},{5,6},{6,7},{8,9},{9,10},{10,11},{11... | collective-permute-start | bytes 405512 | tf_op jit(solution)/shard_map/ppermute | solution.py:21
  96.6 12.1 %collective-permute-start.3 = (bf16[256,2,132]{2,1,0:T(2,128)(2,1)S(1)}, bf16[256,2,132]{2,1,0:T(2,128)(2,1)S(1)}, u32[]{:S(2)}, u32[]{:S(2)}) collective-permute-start(bf16[256,2,132]{2,1,0:T(2,128)(2,1)S(1)} %get-tuple-element.91), channel_id=1, source_target_pairs={{1,0},{2,1},{3,2},{4,3},{5,4},{6,5},{7,6},{9,8},{10,9},{11,10},{12... | collective-permute-start | bytes 405512 | tf_op jit(solution)/shard_map/ppermute | solution.py:24
  116.6 1.7 copy-start.3
  116.6 2.5 %copy-start.4 = (f32[1,36,132]{0,2,1:T(8,128)S(1)}, f32[1,36,132]{0,2,1:T(8,128)}, u32[]{:S(2)}) copy-start(f32[1,36,132]{0,2,1:T(8,128)} %get-tuple-element.135) | copy-start | bytes 57028 | tf_op jit(solution)/shard_map/while
  136.0 1.7 copy-start.3
  136.0 2.5 %copy-start.4 = (f32[1,36,132]{0,2,1:T(8,128)S(1)}, f32[1,36,132]{0,2,1:T(8,128)}, u32[]{:S(2)}) copy-start(f32[1,36,132]{0,2,1:T(8,128)} %get-tuple-element.135) | copy-start | bytes 57028 | tf_op jit(solution)/shard_map/while
  157.1 13.1 %all-to-all-start.3 = ((f32[8,2,128]{2,1,0:T(2,128)}), f32[8,2,128]{2,1,0:T(2,128)S(1)}, u32[]{:S(2)}, u32[]{:S(2)}) async-start(f32[8,2,128]{2,1,0:T(2,128)} %broadcast_select_fusion.1), calls=%async_computation.3 | async-start | bytes 16384 | tf_op jit(solution)/shard_map/all_to_all | solution.py:138
  170.2 12.5 %all-to-all-start.1 = ((f32[8,2,1024]{2,1,0:T(2,128)}), f32[8,2,1024]{2,1,0:T(2,128)S(1)}, u32[]{:S(2)}, u32[]{:S(2)}) async-start(f32[8,2,1024]{2,1,0:T(2,128)} %broadcast_select_fusion), calls=%async_computation.1 | async-start | bytes 131072 | tf_op jit(solution)/shard_map/all_to_all | solution.py:137
where the time goes:
time: 185 us; the launch traced here: 183 us
  local copies, waits for them, and re-layouts  75.2 us (41%)
  other arithmetic  42.9 us (23%)
  starting transfers between devices  31.2 us (17%)
  waiting for transfers between devices  29.1 us (16%)
  loops' own time  4.01 us (2%)
    all_to_all x1, waiting for transfers between devices, per_device(): lax.all_to_all(intensity, 'chan', split_axis=2, concat_axis=0, tiled=True)  22.5 us
    unnamed x16, local copies, waits for them, and re-layouts  21.3 us
    dynamic_update_slice x2, other arithmetic, smooth_tiles(): stacked = lax.map(smooth_block, jnp.arange(chan_blocks, dtype=jnp.int32))  10.8 us
    all_to_all x2, local copies, waits for them, and re-layouts, per_device(): lax.all_to_all(intensity, 'chan', split_axis=2, concat_axis=0, tiled=True)  8.72 us
    add x2, other arithmetic, smooth_block(): sum((weights[offset] * hanning[:, offset:offset + rows_inner, :] for offs...  7.64 us
    concatenate x1, local copies, waits for them, and re-layouts, with_halo(): block = jnp.concatenate([low, block, high], axis=dim)  7.57 us
    slice x3, local copies, waits for them, and re-layouts, with_halo(): lax.slice_in_dim(block, block.shape[dim] - width, None, axis=dim)  6.64 us
    all_to_all x1, starting transfers between devices, per_device(): lax.all_to_all(spectra_slots, 'tile', split_axis=0, concat_axis=0, tiled=...  6.63 us
  transfers between devices with their start and end apart: 8, of which 3 were waited for; matrix products, arithmetic and copies ran while one was open for 31% of the time, Pallas kernels for 0%

commit v1 on v0

v1 whole, which is shorter than its diff:
```python
import functools

import jax
import jax.numpy as jnp
import numpy as np
from jax import lax
from jax.experimental import pallas as pl
from jax.experimental.pallas import tpu as pltpu
from jax.sharding import PartitionSpec as P

BCH = 128
BPIX = 32
CAP = 2
SRC_DEV = 16
SIGMA = 1.5
KC = 8
MESH = pl.DeviceIdType.MESH
F32 = jnp.float32
BF16 = jnp.bfloat16


def gauss_taps():
    off = np.arange(-2, 3).astype(np.float32)
    raw = np.exp(-off * off / np.float32(2.0 * SIGMA * SIGMA))
    g = (raw / raw.sum()).astype(np.float32)
    return [float(g[2]), float(g[3]), float(g[4])]


def split_taps(taps):
    hi = [float(np.float32(np.asarray(v, dtype=jnp.bfloat16))) for v in taps]
    lo = [v - h for v, h in zip(taps, hi)]
    return hi, lo


def banded(dist, same, taps):
    value = jnp.where(dist == 0, taps[0], jnp.where(dist == 1, taps[1], jnp.where(dist == 2, taps[2], 0.0)))
    return jnp.where(same, value, 0.0).astype(BF16)


def iota(shape, dim):
    return lax.broadcasted_iota(jnp.int32, shape, dim)


def kernel(
    n_chan, n_tile, send_count,
    x_ref, pick_ref, owner_ref, source_ref, low_ref, high_ref,
    maps_ref, spec_ref, out_ref,
    amat, bmat, up_out, dn_out, top_in, bot_in, zs, stage, tile_low, tile_high, rep,
    moments, colsum, msg, rcv,
    halo_send, halo_recv, edge_send, edge_recv, data_send, data_recv, own_send, own_recv,
):
    t = lax.axis_index("tile")
    c = lax.axis_index("chan")
    nch, rows, cols = x_ref.shape
    nk = nch // KC
    nq = n_chan * nch // BCH
    ny = n_chan // 2
    taps = gauss_taps()
    hi, lo = split_taps(taps)
    yy, core = c // 2, c % 2
    peers = []
    for dy in range(1, ny):
        for dc in range(2):
            peers.append(lax.rem(yy + dy, ny) * 2 + lax.rem(core + dc, 2))
    peers.append(yy * 2 + 1 - core)
    tiles = [lax.rem(t + d, n_tile) for d in range(1, n_tile)]

    barrier = pltpu.get_barrier_semaphore()
    for p in peers:
        pl.semaphore_signal(barrier, inc=1, device_id=(p, t), device_id_type=MESH)
    for p in tiles:
        pl.semaphore_signal(barrier, inc=1, device_id=(c, p), device_id_type=MESH)

    m = KC * rows

    def chunk_at(p):
        return jnp.where(p == 0, 0, jnp.where(p == 1, nk - 1, p - 1))

    srow, scol = iota((32, m), 0), iota((32, m), 1)
    within = lax.rem(srow, 16)
    wanted = lax.div(within, 2) * rows + lax.rem(within, 2) + jnp.where(srow >= 16, rows - 2, 0)
    select = jnp.where(scol == wanted, 1.0, 0.0).astype(BF16)

    def pack(p, carry):
        k = chunk_at(p)
        x = x_ref[pl.ds(k * KC, KC)].reshape(m, cols)
        picked = jnp.dot(select, x, preferred_element_type=F32).astype(BF16)
        up_out[pl.ds(pl.multiple_of(p * 16, 16), 16), :] = picked[:16]
        dn_out[pl.ds(pl.multiple_of(p * 16, 16), 16), :] = picked[16:]
        return carry

    lax.fori_loop(0, nk, pack, 0)

    arow, acol = iota((m, m), 0), iota((m, m), 1)
    same = lax.div(arow, rows) == lax.div(acol, rows)
    amat[0] = banded(jnp.abs(arow - acol), same, hi)
    amat[1] = banded(jnp.abs(arow - acol), same, lo)
    brow, bcol = iota((m, 64), 0), iota((m, 64), 1)
    inner = lax.rem(bcol, 16)
    place = lax.rem(inner, 2) + jnp.where(lax.rem(bcol, 32) >= 16, rows, -2)
    same = lax.div(inner, 2) == lax.div(brow, rows)
    dist = jnp.abs(lax.rem(brow, rows) - place)
    bmat[...] = jnp.where(bcol < 32, banded(dist, same, hi).astype(F32), banded(dist, same, lo).astype(F32)).astype(BF16)

    @pl.when(t == 0)
    def _():
        top_in[...] = jnp.zeros_like(top_in)

    @pl.when(t == n_tile - 1)
    def _():
        bot_in[...] = jnp.zeros_like(bot_in)

    @pl.when(c == 0)
    def _():
        zs[0] = jnp.zeros((rows, cols), F32)

    @pl.when(c == n_chan - 1)
    def _():
        zs[nch + 1] = jnp.zeros((rows, cols), F32)

    pl.semaphore_wait(barrier, len(peers) + len(tiles))

    def halo(direction, i):
        part = pl.ds(i * 32, 32)
        src, dst = (up_out, bot_in) if direction == 0 else (dn_out, top_in)
        target = lax.max(t - 1, 0) if direction == 0 else lax.min(t + 1, n_tile - 1)
        return pltpu.make_async_remote_copy(
            src_ref=src.at[part, :], dst_ref=dst.at[part, :],
            send_sem=halo_send.at[direction, i], recv_sem=halo_recv.at[direction, i],
            device_id=(c, target), device_id_type=MESH,
        )

    nm = nk // 2
    for i in range(nm):
        @pl.when(t > 0)
        def _():
            halo(0, i).start()

        @pl.when(t < n_tile - 1)
        def _():
            halo(1, i).start()

    def wait_halo(i):
        @pl.when(t < n_tile - 1)
        def _():
            halo(0, i).wait_recv()

        @pl.when(t > 0)
        def _():
            halo(1, i).wait_recv()

    def row_pass(p, carry):
        k = chunk_at(p)
        x = x_ref[pl.ds(k * KC, KC)].reshape(m, cols)
        part = pl.ds(pl.multiple_of(p * 16, 16), 16)
        rim = jnp.concatenate([top_in[part, :], bot_in[part, :]] * 2, axis=0)
        z = jnp.dot(amat[0], x, preferred_element_type=F32)
        z += jnp.dot(amat[1], x, preferred_element_type=F32)
        z += jnp.dot(bmat[...], rim, preferred_element_type=F32)
        zs[pl.ds(k * KC + 1, KC)] = z.reshape(KC, rows, cols)
        return carry

    def edge(direction):
        src, dst = (1, nch + 1) if direction == 0 else (nch, 0)
        target = lax.max(c - 1, 0) if direction == 0 else lax.min(c + 1, n_chan - 1)
        return pltpu.make_async_remote_copy(
            src_ref=zs.at[src], dst_ref=zs.at[dst],
            send_sem=edge_send.at[direction], recv_sem=edge_recv.at[direction],
            device_id=(target, t), device_id_type=MESH,
        )

    def data(slot, source, target, k):
        return pltpu.make_async_remote_copy(
            src_ref=stage.at[target, pl.ds(k * KC, KC)],
            dst_ref=out_ref.at[pl.ds(source * nch + k * KC, KC)],
            send_sem=data_send.at[slot, k], recv_sem=data_recv.at[source, k],
            device_id=(target, t), device_id_type=MESH,
        )

    lane = iota((rows, cols), 1)

    def finish(k, carry):
        def one(i, carry):
            ch = k * KC + i
            h = 0.5 * zs[ch + 1] + 0.25 * (zs[ch] + zs[ch + 2])
            near = jnp.where(lane >= 1, pltpu.roll(h, 1, 1), 0.0) + jnp.where(
                lane < cols - 1, pltpu.roll(h, cols - 1, 1), 0.0
            )
            far = jnp.where(lane >= 2, pltpu.roll(h, 2, 1), 0.0) + jnp.where(
                lane < cols - 2, pltpu.roll(h, cols - 2, 1), 0.0
            )
            res = (taps[0] * h + taps[1] * near + taps[2] * far).astype(BF16)
            width = cols // n_chan
            for j in range(n_chan):
                stage[j, ch] = res[:, j * width : (j + 1) * width]
            return carry

        lax.fori_loop(0, KC, one, 0, unroll=2)
        for slot, p in enumerate(peers):
            data(slot, c, p, k).start()
        out_ref[pl.ds(c * nch + k * KC, KC)] = stage[c, pl.ds(k * KC, KC)]
        return carry

    wait_halo(0)
    lax.fori_loop(0, 2, row_pass, 0)

    @pl.when(c > 0)
    def _():
        edge(0).start()

    @pl.when(c < n_chan - 1)
    def _():
        edge(1).start()

    for i in range(1, nm):
        wait_halo(i)
        lax.fori_loop(2 * i, 2 * i + 2, row_pass, 0)
        lax.fori_loop(max(1, 2 * i - 2), 2 * i if i < nm - 1 else 2 * i + 1, finish, 0)

    @pl.when(c < n_chan - 1)
    def _():
        edge(0).wait_recv()

    @pl.when(c > 0)
    def _():
        edge(1).wait_recv()

    lax.fori_loop(0, 2, lambda i, carry: finish(i * (nk - 1), carry), 0)

    width = cols // n_chan
    per = width // BPIX
    r, l = iota((rows, width), 0), iota((rows, width), 1)
    group = lax.div(l, BPIX)
    turn = lax.rem(group - lax.rem(r, per) + per, per)
    for q in range(nq):
        tile_low[q] = jnp.zeros((rows, width), jnp.int32)
        tile_high[q] = jnp.zeros((rows, width), jnp.int32)
    picks = [pick_ref[0, 0, s] for s in range(send_count)]
    owners = [owner_ref[0, 0, s] for s in range(send_count)]
    sources = [source_ref[0, 0, s] for s in range(send_count)]
    slots = []
    for s in range(send_count):
        rank = jnp.int32(0)
        for e in range(s):
            rank = rank + jnp.where(owners[e] == owners[s], 1, 0)
        slots.append(owners[s] * CAP + rank)
    qs = [lax.div(p, per) for p in picks]
    vs = [lax.rem(p, per) for p in picks]
    for s in range(send_count):
        for ends_ref, grid in ((low_ref, tile_low), (high_ref, tile_high)):
            for a in range(rows // per):
                line = ends_ref[0, 0, pl.ds(s, 1), pl.ds(a * width, width)]
                rep[pl.ds(a * per, per), :] = jnp.broadcast_to(line, (per, width))
            base = rep[...]
            value = base
            for i in range(1, per):
                value = jnp.where(turn == i, pltpu.roll(base, i * BPIX, 1), value)
            for q in range(nq):
                hit = (group == vs[s]) & (qs[s] == q)
                grid[q] = jnp.where(hit, value, grid[q])

    moments[...] = jnp.zeros_like(moments)
    chans = iota((KC, rows, width), 0)

    def measure(source, k):
        base = pl.multiple_of(source * nch + k * KC, KC)
        q = lax.div(base, BCH)
        v = out_ref[pl.ds(base, KC)].astype(F32)
        pos = chans + lax.rem(base, BCH)
        inside = (tile_low[q][None] <= pos) & (pos < tile_high[q][None])
        v = jnp.where(inside, v, 0.0)
        moments[q] += jnp.sum(v, axis=0)
        colsum[pl.ds(base, KC), :] = jnp.sum(v, axis=1)

    def order(i):
        return jnp.where(i < nk - 2, i + 1, jnp.where(i == nk - 2, 0, nk - 1))

    def own(k, carry):
        measure(c, k)
        return carry

    lax.fori_loop(0, nk, own, 0)

    def arrive_same(i, carry):
        k = order(i)
        data(len(peers) - 1, peers[-1], c, k).wait_recv()
        measure(peers[-1], k)
        return carry

    lax.fori_loop(0, nk, arrive_same, 0)

    def arrive(i, carry):
        k = order(i)
        for slot, p in enumerate(peers[:-1]):
            data(slot, p, c, k).wait_recv()
            measure(p, k)
        return carry

    lax.fori_loop(0, nk, arrive, 0)

    fold = jnp.where(lax.div(iota((rows // per, rows), 1), per) == iota((rows // per, rows), 0), 1.0, 0.0)
    maps = []
    for s in range(send_count):
        total = jnp.zeros((rows, width), F32)
        for q in range(nq):
            total = jnp.where((group == vs[s]) & (qs[s] == q), moments[q], total)
        step = BPIX
        while step < width:
            total = total + pltpu.roll(total, step, 1)
            step *= 2
        total = jnp.where(group == lax.rem(r, per), total, 0.0)
        maps.append(jnp.dot(fold, total, precision=lax.Precision.HIGHEST, preferred_element_type=F32))
    entries = n_tile * CAP
    er, el = iota((entries, width), 0), iota((entries, width), 1)
    eg = lax.div(el, BPIX)
    spectra = jnp.zeros((entries, BCH), F32)
    tags = jnp.zeros((entries, width), F32)
    for q in range(nq):
        chosen = jnp.zeros((entries, width), F32)
        for s in range(send_count):
            chosen = jnp.where((er == slots[s]) & (eg == vs[s]) & (qs[s] == q), 1.0, chosen)
        spectra += lax.dot_general(
            chosen, colsum[pl.ds(q * BCH, BCH), :], (((1,), (1,)), ((), ())),
            precision=lax.Precision.HIGHEST, preferred_element_type=F32,
        )
    for s in range(send_count):
        tags = jnp.where(er == slots[s], (sources[s] * nq + qs[s]).astype(F32), tags)
    for o in range(n_tile):
        for n in range(CAP):
            total = jnp.zeros((rows // per, width), F32)
            for s in range(send_count):
                total = jnp.where(slots[s] == o * CAP + n, maps[s], total)
            msg[o, pl.ds(n * 8, 8), :] = total
        part = slice(o * CAP, o * CAP + CAP)
        msg[o, pl.ds(16, 8), :] = jnp.concatenate(
            [spectra[part], tags[part], jnp.zeros((4, width), F32)], axis=0
        )

    def to_owner(d, source, target):
        return pltpu.make_async_remote_copy(
            src_ref=msg.at[target], dst_ref=rcv.at[source],
            send_sem=own_send.at[d], recv_sem=own_recv.at[source],
            device_id=(c, target), device_id_type=MESH,
        )

    for d, p in enumerate(tiles):
        to_owner(d, t, p).start()
    rcv[t] = msg[t]

    for i in range(nm):
        @pl.when(t > 0)
        def _():
            halo(0, i).wait_send()

        @pl.when(t < n_tile - 1)
        def _():
            halo(1, i).wait_send()

    @pl.when(c > 0)
    def _():
        edge(0).wait_send()

    @pl.when(c < n_chan - 1)
    def _():
        edge(1).wait_send()

    def left(k, carry):
        for slot, p in enumerate(peers):
            data(slot, c, p, k).wait_send()
        return carry

    lax.fori_loop(0, nk, left, 0)
    for d, p in enumerate(tiles):
        to_owner(d, t, p).wait_send()
    for d, p in enumerate(tiles):
        to_owner(d, p, p).wait_recv()

    maps_ref[...] = rcv[:, :16, :]
    which = iota((SRC_DEV, width), 0) * nq
    totals = [jnp.zeros((SRC_DEV, BCH), F32) for _ in range(nq)]
    for i in range(n_tile):
        for n in range(CAP):
            line = rcv[i, pl.ds(16 + n, 1), :]
            tag = rcv[i, pl.ds(18 + n, 1), :]
            for q in range(nq):
                totals[q] = totals[q] + jnp.where(tag == (which + q).astype(F32), line, 0.0)
    for q in range(nq):
        spec_ref[:, pl.ds(q * BCH, BCH)] = totals[q]


def solution(mesh):
    n_chan, n_tile = mesh.shape["chan"], mesh.shape["tile"]

    def step(intensity, block_pick, owner_tile, source_index, mask_low, mask_high):
        nch, rows, cols = intensity.shape
        width = cols // n_chan
        send_count = block_pick.shape[-1]
        total = nch * n_chan
        nq = total // BCH
        nk = nch // KC
        vmem = pl.BlockSpec(memory_space=pltpu.VMEM)
        smem = pl.BlockSpec(memory_space=pltpu.SMEM)
        dma = pltpu.SemaphoreType.DMA
        maps, spectra, smoothed = pl.pallas_call(
            functools.partial(kernel, n_chan, n_tile, send_count),
            out_shape=(
                jax.ShapeDtypeStruct((n_tile, CAP * 8, 128), F32),
                jax.ShapeDtypeStruct((SRC_DEV, total), F32),
                jax.ShapeDtypeStruct((total, rows, width), BF16),
            ),
            in_specs=[vmem, smem, smem, smem, vmem, vmem],
            out_specs=(vmem, vmem, vmem),
            scratch_shapes=[
                pltpu.VMEM((2, KC * rows, KC * rows), BF16),
                pltpu.VMEM((KC * rows, 64), BF16),
                pltpu.VMEM((nch * 2, cols), BF16),
                pltpu.VMEM((nch * 2, cols), BF16),
                pltpu.VMEM((nch * 2, cols), BF16),
                pltpu.VMEM((nch * 2, cols), BF16),
                pltpu.VMEM((nch + 2, rows, cols), F32),
                pltpu.VMEM((n_chan, nch, rows, width), BF16),
                pltpu.VMEM((nq, rows, width), jnp.int32),
                pltpu.VMEM((nq, rows, width), jnp.int32),
                pltpu.VMEM((rows, width), jnp.int32),
                pltpu.VMEM((nq, rows, width), F32),
                pltpu.VMEM((total, width), F32),
                pltpu.VMEM((n_tile, 24, width), F32),
                pltpu.VMEM((n_tile, 24, width), F32),
                dma((2, nk // 2)), dma((2, nk // 2)), dma((2,)), dma((2,)),
                dma((n_chan - 1, nk)), dma((n_chan, nk)),
                dma((n_tile - 1,)), dma((n_tile,)),
            ],
            compiler_params=pltpu.CompilerParams(
                collective_id=0, has_side_effects=True, vmem_limit_bytes=48 * 1024 * 1024
            ),
        )(intensity, block_pick, owner_tile, source_index, mask_low, mask_high)
        return (
            maps.reshape(1, 1, n_tile, CAP, 8 * 128),
            spectra.reshape(1, 1, SRC_DEV, total),
            smoothed,
        )

    return jax.shard_map(
        step,
        mesh=mesh,
        in_specs=(
            P("chan", "tile", None),
            P("tile", "chan", None),
            P("tile", "chan", None),
            P("tile", "chan", None),
            P("tile", "chan", None, None),
            P("tile", "chan", None, None),
        ),
        out_specs=(
            P("tile", "chan", None, None, None),
            P("tile", "chan", None, None),
            P(None, "tile", "chan"),
        ),
        check_vma=False,
    )
```

time: 185 us -> 51.3 us (0.28)
  local copies, waits for them, and re-layouts: 75.2 us -> 7.57 us
  other arithmetic: 42.9 us -> 0 us
  Pallas kernels: 0 us -> 42.8 us
  starting transfers between devices: 31.2 us -> 0 us
  waiting for transfers between devices: 29.1 us -> 0 us
  loops' own time: 4.01 us -> 0 us
    pallas_call x0 -> x1, Pallas kernels: none -> 42.8 us  [step(): pl.pallas_call(functools.partial(kernel, n_chan, n_tile, send_count), out...]
    all_to_all x4 -> x0, waiting for transfers between devices: 29.1 us -> none  [the longest x1 22.5 us: per_device(): lax.all_to_all(intensity, 'chan', split_axis=2, concat_axis=0, tiled=True)]
    all_to_all x4 -> x0, starting transfers between devices: 23.2 us -> none  [the longest x1 6.63 us: per_device(): lax.all_to_all(spectra_slots, 'tile', split_axis=0, concat_axis=0, tiled=...]
    unnamed x16 -> x14, local copies, waits for them, and re-layouts: 21.3 us -> 6.91 us
    slice x8 -> x0, local copies, waits for them, and re-layouts: 12.8 us -> none  [the longest x3 6.64 us: with_halo(): lax.slice_in_dim(block, block.shape[dim] - width, None, axis=dim)]
    dynamic_update_slice x2 -> x0, other arithmetic: 10.8 us -> none  [smooth_tiles(): stacked = lax.map(smooth_block, jnp.arange(chan_blocks, dtype=jnp.int32))]
    add x6 -> x0, other arithmetic: 10.4 us -> none  [the longest x2 7.64 us: smooth_block(): sum((weights[offset] * hanning[:, offset:offset + rows_inner, :] for offs...]
    ppermute x4 -> x0, local copies, waits for them, and re-layouts: 8.76 us -> none  [the longest x2 4.4 us: with_halo(): lax.ppermute(lax.slice_in_dim(block, block.shape[dim] - width, None, axis...]
  transfers between devices with their start and end apart: 8 -> 0, of which waited for: 3 -> 0; matrix products, arithmetic and copies ran while one was open for 31% -> 0% of each run, Pallas kernels for 0% -> 0%
where the time goes in v1:
time: 51.3 us; the launch traced here: 51 us
  Pallas kernels  42.8 us (83%)
  local copies, waits for them, and re-layouts  7.57 us (15%)
  between operations  0.65 us (1%)
    pallas_call x1, Pallas kernels, step(): pl.pallas_call(functools.partial(kernel, n_chan, n_tile, send_count), out...  42.8 us
    unnamed x14, local copies, waits for them, and re-layouts  6.91 us

profile of v1, /device:TPU:0, one launch (start us, length us, event | category | flops | bytes accessed | tf_op | source)
XLA Modules:
  0.0 51.0 jit_solution(13795753599068898607)
XLA Ops:
  0.6 0.0 copy-start
  0.6 1.6 %copy-done = bf16[64,32,512]{2,1,0:T(8,128)(2,1)S(1)} copy-done((bf16[64,32,512]{2,1,0:T(8,128)(2,1)S(1)}, bf16[64,32,512]{2,1,0:T(8,128)(2,1)}, u32[]{:S(2)}) %copy-start) | copy-done | bytes 2097176
  2.2 0.0 copy-start.1
  2.2 0.7 %copy-done.1 = s32[1,1,4,1024]{3,2,1,0:T(4,128)S(1)} copy-done((s32[1,1,4,1024]{3,2,1,0:T(4,128)S(1)}, s32[1,1,4,1024]{3,2,1,0:T(4,128)}, u32[]{:S(2)}) %copy-start.1) | copy-done | bytes 16408
  2.9 0.0 copy-start.2
  2.9 0.7 %copy-done.2 = s32[1,1,4,1024]{3,2,1,0:T(4,128)S(1)} copy-done((s32[1,1,4,1024]{3,2,1,0:T(4,128)S(1)}, s32[1,1,4,1024]{3,2,1,0:T(4,128)}, u32[]{:S(2)}) %copy-start.2) | copy-done | bytes 16408
  3.7 0.0 copy-start.3
  3.7 0.7 %copy-done.3 = s32[1,1,4]{2,1,0:T(1,128)S(1)} copy-done((s32[1,1,4]{2,1,0:T(1,128)S(1)}, s32[1,1,4]{2,1,0:T(1,128)}, u32[]{:S(2)}) %copy-start.3) | copy-done | bytes 40
  4.3 0.0 copy-start.4
  4.3 0.7 %copy-done.4 = s32[1,1,4]{2,1,0:T(1,128)S(1)} copy-done((s32[1,1,4]{2,1,0:T(1,128)S(1)}, s32[1,1,4]{2,1,0:T(1,128)}, u32[]{:S(2)}) %copy-start.4) | copy-done | bytes 40
  5.0 0.0 copy-start.5
  5.0 0.7 %copy-done.5 = s32[1,1,4]{2,1,0:T(1,128)S(1)} copy-done((s32[1,1,4]{2,1,0:T(1,128)S(1)}, s32[1,1,4]{2,1,0:T(1,128)}, u32[]{:S(2)}) %copy-start.5) | copy-done | bytes 40
  5.6 42.8 %shard_map.85 = (f32[8,16,128]{2,1,0:T(8,128)S(1)}, f32[16,256]{1,0:T(8,128)S(1)}, bf16[256,32,128]{2,1,0:T(8,128)(2,1)S(1)}) custom-call(bf16[64,32,512]{2,1,0:T(8,128)(2,1)S(1)} %copy-done, s32[1,1,4]{2,1,0:T(1,128)S(1)} %copy-done.3, s32[1,1,4]{2,1,0:T(1,128)S(1)} %copy-done.4, s32[1,1,4]{2,1,0:T(1,128)S(1)} %copy-done.5, ...), custom_call_target="tpu_custom_call" | custom-call | tf_op jit(solution)/shard_map/pallas_call | solution.py:404
  48.4 0.7 %reshape.12 = f32[1,1,8,2,1024]{4,3,2,1,0:T(2,128)} reshape(f32[8,16,128]{2,1,0:T(8,128)S(1)} %get-tuple-element.6) | data formatting | bytes 131072 | tf_op jit(solution)/shard_map/reshape | solution.py:438
  49.1 0.6 %copy.11 = f32[1,1,16,256]{3,2,1,0:T(8,128)} copy(f32[1,1,16,256]{3,2,1,0:T(8,128)S(1)} %bitcast.1) | data formatting | bytes 32768
  49.7 1.3 %copy.12 = bf16[256,32,128]{2,1,0:T(8,128)(2,1)} copy(bf16[256,32,128]{2,1,0:T(8,128)(2,1)S(1)} %get-tuple-element.14) | data formatting | bytes 4194304
Async XLA Ops:
  0.6 1.6 %copy-start = (bf16[64,32,512]{2,1,0:T(8,128)(2,1)S(1)}, bf16[64,32,512]{2,1,0:T(8,128)(2,1)}, u32[]{:S(2)}) copy-start(bf16[64,32,512]{2,1,0:T(8,128)(2,1)} %x_ref.1) | copy-start | bytes 6291460
  2.2 0.7 %copy-start.1 = (s32[1,1,4,1024]{3,2,1,0:T(4,128)S(1)}, s32[1,1,4,1024]{3,2,1,0:T(4,128)}, u32[]{:S(2)}) copy-start(s32[1,1,4,1024]{3,2,1,0:T(4,128)} %low_ref.1) | copy-start | bytes 49156
  2.9 0.7 %copy-start.2 = (s32[1,1,4,1024]{3,2,1,0:T(4,128)S(1)}, s32[1,1,4,1024]{3,2,1,0:T(4,128)}, u32[]{:S(2)}) copy-start(s32[1,1,4,1024]{3,2,1,0:T(4,128)} %high_ref.1) | copy-start | bytes 49156
  3.7 0.7 %copy-start.3 = (s32[1,1,4]{2,1,0:T(1,128)S(1)}, s32[1,1,4]{2,1,0:T(1,128)}, u32[]{:S(2)}) copy-start(s32[1,1,4]{2,1,0:T(1,128)} %pick_ref.1) | copy-start | bytes 52
  4.3 0.7 %copy-start.4 = (s32[1,1,4]{2,1,0:T(1,128)S(1)}, s32[1,1,4]{2,1,0:T(1,128)}, u32[]{:S(2)}) copy-start(s32[1,1,4]{2,1,0:T(1,128)} %owner_ref.1) | copy-start | bytes 52
  5.0 0.7 %copy-start.5 = (s32[1,1,4]{2,1,0:T(1,128)S(1)}, s32[1,1,4]{2,1,0:T(1,128)}, u32[]{:S(2)}) copy-start(s32[1,1,4]{2,1,0:T(1,128)} %source_ref.1) | copy-start | bytes 52

commit v2 on v1

--- a/solution.py
+++ b/solution.py
@@ -43,11 +43,12 @@
 
 def kernel(
     n_chan, n_tile, send_count,
+    x_hbm, pick_hbm, owner_hbm, source_hbm, low_hbm, high_hbm,
+    maps_ref, spec_ref, out_ref,
     x_ref, pick_ref, owner_ref, source_ref, low_ref, high_ref,
-    maps_ref, spec_ref, out_ref,
     amat, bmat, up_out, dn_out, top_in, bot_in, zs, stage, tile_low, tile_high, rep,
-    moments, colsum, msg, rcv,
-    halo_send, halo_recv, edge_send, edge_recv, data_send, data_recv, own_send, own_recv,
+    moments, colsum, msg, rcv, pick_mat,
+    x_sem, arg_sem, halo_send, halo_recv, edge_send, edge_recv, data_send, data_recv, own_send, own_recv,
 ):
     t = lax.axis_index("tile")
     c = lax.axis_index("chan")
@@ -65,31 +66,71 @@
     peers.append(yy * 2 + 1 - core)
     tiles = [lax.rem(t + d, n_tile) for d in range(1, n_tile)]
 
+    def fetch(p):
+        part = pl.ds(p * KC, KC)
+        return pltpu.make_async_copy(x_hbm.at[part], x_ref.at[part], x_sem.at[p])
+
+    small = [
+        pltpu.make_async_copy(src, dst, arg_sem.at[i])
+        for i, (src, dst) in enumerate((
+            (pick_hbm, pick_ref), (owner_hbm, owner_ref), (source_hbm, source_ref),
+            (low_hbm, low_ref), (high_hbm, high_ref),
+        ))
+    ]
     barrier = pltpu.get_barrier_semaphore()
     for p in peers:
         pl.semaphore_signal(barrier, inc=1, device_id=(p, t), device_id_type=MESH)
     for p in tiles:
         pl.semaphore_signal(barrier, inc=1, device_id=(c, p), device_id_type=MESH)
 
+    for p in range(nk):
+        fetch(p).start()
+    for copy in small:
+        copy.start()
     m = KC * rows
-
-    def chunk_at(p):
-        return jnp.where(p == 0, 0, jnp.where(p == 1, nk - 1, p - 1))
 
     srow, scol = iota((32, m), 0), iota((32, m), 1)
     within = lax.rem(srow, 16)
     wanted = lax.div(within, 2) * rows + lax.rem(within, 2) + jnp.where(srow >= 16, rows - 2, 0)
     select = jnp.where(scol == wanted, 1.0, 0.0).astype(BF16)
 
-    def pack(p, carry):
-        k = chunk_at(p)
+    def pack(k):
+        fetch(k).wait()
         x = x_ref[pl.ds(k * KC, KC)].reshape(m, cols)
         picked = jnp.dot(select, x, preferred_element_type=F32).astype(BF16)
-        up_out[pl.ds(pl.multiple_of(p * 16, 16), 16), :] = picked[:16]
-        dn_out[pl.ds(pl.multiple_of(p * 16, 16), 16), :] = picked[16:]
-        return carry
-
-    lax.fori_loop(0, nk, pack, 0)
+        up_out[pl.ds(pl.multiple_of(k * 16, 16), 16), :] = picked[:16]
+        dn_out[pl.ds(pl.multiple_of(k * 16, 16), 16), :] = picked[16:]
+
+    pack(0)
+    pl.semaphore_wait(barrier, len(peers) + len(tiles))
+
+    def halo(direction, i):
+        part = pl.ds(i * 16, 16)
+        src, dst = (up_out, bot_in) if direction == 0 else (dn_out, top_in)
+        target = lax.max(t - 1, 0) if direction == 0 else lax.min(t + 1, n_tile - 1)
+        return pltpu.make_async_remote_copy(
+            src_ref=src.at[part, :], dst_ref=dst.at[part, :],
+            send_sem=halo_send.at[direction, i], recv_sem=halo_recv.at[direction, i],
+            device_id=(c, target), device_id_type=MESH,
+        )
+
+    def send_halo(i):
+        @pl.when(t > 0)
+        def _():
+            halo(0, i).start()
+
+        @pl.when(t < n_tile - 1)
+        def _():
+            halo(1, i).start()
+
+    send_halo(0)
+
+    def pack_on(k, carry):
+        pack(k)
+        send_halo(k)
+        return carry
+
+    lax.fori_loop(1, nk, pack_on, 0)
 
     arow, acol = iota((m, m), 0), iota((m, m), 1)
     same = lax.div(arow, rows) == lax.div(acol, rows)
@@ -118,28 +159,6 @@
     def _():
         zs[nch + 1] = jnp.zeros((rows, cols), F32)
 
-    pl.semaphore_wait(barrier, len(peers) + len(tiles))
-
-    def halo(direction, i):
-        part = pl.ds(i * 32, 32)
-        src, dst = (up_out, bot_in) if direction == 0 else (dn_out, top_in)
-        target = lax.max(t - 1, 0) if direction == 0 else lax.min(t + 1, n_tile - 1)
-        return pltpu.make_async_remote_copy(
-            src_ref=src.at[part, :], dst_ref=dst.at[part, :],
-            send_sem=halo_send.at[direction, i], recv_sem=halo_recv.at[direction, i],
-            device_id=(c, target), device_id_type=MESH,
-        )
-
-    nm = nk // 2
-    for i in range(nm):
-        @pl.when(t > 0)
-        def _():
-            halo(0, i).start()
-
-        @pl.when(t < n_tile - 1)
-        def _():
-            halo(1, i).start()
-
     def wait_halo(i):
         @pl.when(t < n_tile - 1)
         def _():
@@ -149,16 +168,15 @@
         def _():
             halo(1, i).wait_recv()
 
-    def row_pass(p, carry):
-        k = chunk_at(p)
+    def row_pass(k):
+        wait_halo(k)
         x = x_ref[pl.ds(k * KC, KC)].reshape(m, cols)
-        part = pl.ds(pl.multiple_of(p * 16, 16), 16)
+        part = pl.ds(pl.multiple_of(k * 16, 16), 16)
         rim = jnp.concatenate([top_in[part, :], bot_in[part, :]] * 2, axis=0)
         z = jnp.dot(amat[0], x, preferred_element_type=F32)
         z += jnp.dot(amat[1], x, preferred_element_type=F32)
         z += jnp.dot(bmat[...], rim, preferred_element_type=F32)
         zs[pl.ds(k * KC + 1, KC)] = z.reshape(KC, rows, cols)
-        return carry
 
     def edge(direction):
         src, dst = (1, nch + 1) if direction == 0 else (nch, 0)
@@ -179,7 +197,7 @@
 
     lane = iota((rows, cols), 1)
 
-    def finish(k, carry):
+    def finish(k):
         def one(i, carry):
             ch = k * KC + i
             h = 0.5 * zs[ch + 1] + 0.25 * (zs[ch] + zs[ch + 2])
@@ -199,24 +217,28 @@
         for slot, p in enumerate(peers):
             data(slot, c, p, k).start()
         out_ref[pl.ds(c * nch + k * KC, KC)] = stage[c, pl.ds(k * KC, KC)]
-        return carry
-
-    wait_halo(0)
-    lax.fori_loop(0, 2, row_pass, 0)
+
+    def first(k, carry):
+        row_pass(k)
+        return carry
+
+    def both(k, carry):
+        row_pass(k)
+        finish(k - 1)
+        return carry
+
+    lax.fori_loop(0, 2, first, 0)
 
     @pl.when(c > 0)
     def _():
         edge(0).start()
 
+    lax.fori_loop(2, nk, both, 0)
+
     @pl.when(c < n_chan - 1)
     def _():
         edge(1).start()
 
-    for i in range(1, nm):
-        wait_halo(i)
-        lax.fori_loop(2 * i, 2 * i + 2, row_pass, 0)
-        lax.fori_loop(max(1, 2 * i - 2), 2 * i if i < nm - 1 else 2 * i + 1, finish, 0)
-
     @pl.when(c < n_chan - 1)
     def _():
         edge(0).wait_recv()
@@ -225,8 +247,14 @@
     def _():
         edge(1).wait_recv()
 
-    lax.fori_loop(0, 2, lambda i, carry: finish(i * (nk - 1), carry), 0)
-
+    def last(i, carry):
+        finish(i * (nk - 1))
+        return carry
+
+    lax.fori_loop(0, 2, last, 0)
+
+    for copy in small:
+        copy.wait()
     width = cols // n_chan
     per = width // BPIX
     r, l = iota((rows, width), 0), iota((rows, width), 1)
@@ -259,6 +287,21 @@
                 hit = (group == vs[s]) & (qs[s] == q)
                 grid[q] = jnp.where(hit, value, grid[q])
 
+    entries = n_tile * CAP
+    er = iota((entries, width), 0)
+    eg = lax.div(iota((entries, width), 1), BPIX)
+    tags = jnp.zeros((entries, width), F32)
+    for q in range(nq):
+        chosen = jnp.zeros((entries, width), F32)
+        for s in range(send_count):
+            chosen = jnp.where((er == slots[s]) & (eg == vs[s]) & (qs[s] == q), 1.0, chosen)
+        pick_mat[q] = jnp.concatenate([chosen, chosen], axis=1).astype(BF16)
+    for s in range(send_count):
+        tags = jnp.where(er == slots[s], (sources[s] * nq + qs[s]).astype(F32), tags)
+    for o in range(n_tile):
+        msg[o, pl.ds(16, 8), :] = jnp.concatenate(
+            [tags[o * CAP : o * CAP + CAP], jnp.zeros((6, width), F32)], axis=0
+        )
     moments[...] = jnp.zeros_like(moments)
     chans = iota((KC, rows, width), 0)
 
@@ -298,43 +341,39 @@
 
     lax.fori_loop(0, nk, arrive, 0)
 
-    fold = jnp.where(lax.div(iota((rows // per, rows), 1), per) == iota((rows // per, rows), 0), 1.0, 0.0)
+    blocks = {}
+    lines = iota((rows // per, width), 1)
+    lane_group = lax.div(lines, BPIX)
+    for q in range(nq):
+        strips = [moments[q, pl.ds(j, rows // per, stride=per), :] for j in range(per)]
+        for v in range(per):
+            total = jnp.zeros((rows // per, width), F32)
+            for j in range(per):
+                turned = strips[j] if j == v else pltpu.roll(strips[j], (j - v) % per * BPIX, 1)
+                total = jnp.where(lane_group == j, turned, total)
+            blocks[q, v] = total
     maps = []
     for s in range(send_count):
-        total = jnp.zeros((rows, width), F32)
-        for q in range(nq):
-            total = jnp.where((group == vs[s]) & (qs[s] == q), moments[q], total)
-        step = BPIX
-        while step < width:
-            total = total + pltpu.roll(total, step, 1)
-            step *= 2
-        total = jnp.where(group == lax.rem(r, per), total, 0.0)
-        maps.append(jnp.dot(fold, total, precision=lax.Precision.HIGHEST, preferred_element_type=F32))
-    entries = n_tile * CAP
-    er, el = iota((entries, width), 0), iota((entries, width), 1)
-    eg = lax.div(el, BPIX)
+        total = jnp.zeros((rows // per, width), F32)
+        for (q, v), block in blocks.items():
+            total = jnp.where(picks[s] == q * per + v, block, total)
+        maps.append(total)
     spectra = jnp.zeros((entries, BCH), F32)
-    tags = jnp.zeros((entries, width), F32)
     for q in range(nq):
-        chosen = jnp.zeros((entries, width), F32)
-        for s in range(send_count):
-            chosen = jnp.where((er == slots[s]) & (eg == vs[s]) & (qs[s] == q), 1.0, chosen)
+        sums = colsum[pl.ds(q * BCH, BCH), :]
+        high = sums.astype(BF16)
+        low = (sums - high.astype(F32)).astype(BF16)
         spectra += lax.dot_general(
-            chosen, colsum[pl.ds(q * BCH, BCH), :], (((1,), (1,)), ((), ())),
-            precision=lax.Precision.HIGHEST, preferred_element_type=F32,
-        )
-    for s in range(send_count):
-        tags = jnp.where(er == slots[s], (sources[s] * nq + qs[s]).astype(F32), tags)
+            pick_mat[q], jnp.concatenate([high, low], axis=1), (((1,), (1,)), ((), ())),
+            preferred_element_type=F32,
+        )
     for o in range(n_tile):
         for n in range(CAP):
             total = jnp.zeros((rows // per, width), F32)
             for s in range(send_count):
                 total = jnp.where(slots[s] == o * CAP + n, maps[s], total)
             msg[o, pl.ds(n * 8, 8), :] = total
-        part = slice(o * CAP, o * CAP + CAP)
-        msg[o, pl.ds(16, 8), :] = jnp.concatenate(
-            [spectra[part], tags[part], jnp.zeros((4, width), F32)], axis=0
-        )
+        msg[o, pl.ds(16 + CAP, CAP), :] = spectra[o * CAP : o * CAP + CAP]
 
     def to_owner(d, source, target):
         return pltpu.make_async_remote_copy(
@@ -347,7 +386,7 @@
         to_owner(d, t, p).start()
     rcv[t] = msg[t]
 
-    for i in range(nm):
+    def halo_left(i, carry):
         @pl.when(t > 0)
         def _():
             halo(0, i).wait_send()
@@ -355,6 +394,10 @@
         @pl.when(t < n_tile - 1)
         def _():
             halo(1, i).wait_send()
+
+        return carry
+
+    lax.fori_loop(0, nk, halo_left, 0)
 
     @pl.when(c > 0)
     def _():
@@ -380,8 +423,8 @@
     totals = [jnp.zeros((SRC_DEV, BCH), F32) for _ in range(nq)]
     for i in range(n_tile):
         for n in range(CAP):
-            line = rcv[i, pl.ds(16 + n, 1), :]
-            tag = rcv[i, pl.ds(18 + n, 1), :]
+            line = rcv[i, pl.ds(18 + n, 1), :]
+            tag = rcv[i, pl.ds(16 + n, 1), :]
             for q in range(nq):
                 totals[q] = totals[q] + jnp.where(tag == (which + q).astype(F32), line, 0.0)
     for q in range(nq):
@@ -399,7 +442,7 @@
         nq = total // BCH
         nk = nch // KC
         vmem = pl.BlockSpec(memory_space=pltpu.VMEM)
-        smem = pl.BlockSpec(memory_space=pltpu.SMEM)
+        hbm = pl.BlockSpec(memory_space=pltpu.HBM)
         dma = pltpu.SemaphoreType.DMA
         maps, spectra, smoothed = pl.pallas_call(
             functools.partial(kernel, n_chan, n_tile, send_count),
@@ -408,9 +451,15 @@
                 jax.ShapeDtypeStruct((SRC_DEV, total), F32),
                 jax.ShapeDtypeStruct((total, rows, width), BF16),
             ),
-            in_specs=[vmem, smem, smem, smem, vmem, vmem],
+            in_specs=[hbm] * 6,
             out_specs=(vmem, vmem, vmem),
             scratch_shapes=[
+                pltpu.VMEM((nch, rows, cols), BF16),
+                pltpu.SMEM((1, 1, send_count), jnp.int32),
+                pltpu.SMEM((1, 1, send_count), jnp.int32),
+                pltpu.SMEM((1, 1, send_count), jnp.int32),
+                pltpu.VMEM((1, 1, send_count, 8 * 128), jnp.int32),
+                pltpu.VMEM((1, 1, send_count, 8 * 128), jnp.int32),
                 pltpu.VMEM((2, KC * rows, KC * rows), BF16),
                 pltpu.VMEM((KC * rows, 64), BF16),
                 pltpu.VMEM((nch * 2, cols), BF16),
@@ -426,14 +475,15 @@
                 pltpu.VMEM((total, width), F32),
                 pltpu.VMEM((n_tile, 24, width), F32),
                 pltpu.VMEM((n_tile, 24, width), F32),
-                dma((2, nk // 2)), dma((2, nk // 2)), dma((2,)), dma((2,)),
+                pltpu.VMEM((nq, n_tile * CAP, 2 * width), BF16),
+                dma((nk,)), dma((5,)), dma((2, nk)), dma((2, nk)), dma((2,)), dma((2,)),
                 dma((n_chan - 1, nk)), dma((n_chan, nk)),
                 dma((n_tile - 1,)), dma((n_tile,)),
             ],
             compiler_params=pltpu.CompilerParams(
-                collective_id=0, has_side_effects=True, vmem_limit_bytes=48 * 1024 * 1024
+                collective_id=0, has_side_effects=True, vmem_limit_bytes=49152 * 1024
             ),
-        )(intensity, block_pick, owner_tile, source_index, mask_low, mask_high)
+        )(*[pltpu.with_memory_space_constraint(v, pltpu.HBM) for v in (intensity, block_pick, owner_tile, source_index, mask_low, mask_high)])
         return (
             maps.reshape(1, 1, n_tile, CAP, 8 * 128),
             spectra.reshape(1, 1, SRC_DEV, total),

time: 51.3 us -> 45.7 us (0.89)
  local copies, waits for them, and re-layouts: 7.57 us -> 2.59 us
    unnamed x14 -> x2, local copies, waits for them, and re-layouts: 6.91 us -> 1.92 us
where the time goes in v2:
time: 45.7 us; the launch traced here: 45.5 us
  Pallas kernels  42.3 us (93%)
  local copies, waits for them, and re-layouts  2.59 us (6%)
  between operations  0.64 us (1%)
    pallas_call x1, Pallas kernels, step(): pl.pallas_call(functools.partial(kernel, n_chan, n_tile, send_count), out...  42.3 us
    unnamed x2, local copies, waits for them, and re-layouts  1.92 us

profile of v2, /device:TPU:0, one launch (start us, length us, event | category | flops | bytes accessed | tf_op | source)
XLA Modules:
  0.0 45.5 jit_solution(12353395527123053453)
XLA Ops:
  0.6 42.3 %shard_map.85 = (f32[8,16,128]{2,1,0:T(8,128)S(1)}, f32[16,256]{1,0:T(8,128)S(1)}, bf16[256,32,128]{2,1,0:T(8,128)(2,1)S(1)}) custom-call(bf16[64,32,512]{2,1,0:T(8,128)(2,1)} %x_hbm.1, s32[1,1,4]{2,1,0:T(1,128)} %pick_hbm.1, s32[1,1,4]{2,1,0:T(1,128)} %owner_hbm.1, s32[1,1,4]{2,1,0:T(1,128)} %source_hbm.1, s32[1,1,4,1024]{3,2,1,0:T(4,128)} %low_hbm.1, ...), custom_call_target="tpu_custom_call" | custom-call | tf_op jit(solution)/shard_map/pallas_call | solution.py:447
  42.9 0.7 %reshape.12 = f32[1,1,8,2,1024]{4,3,2,1,0:T(2,128)} reshape(f32[8,16,128]{2,1,0:T(8,128)S(1)} %get-tuple-element.6) | data formatting | bytes 131072 | tf_op jit(solution)/shard_map/reshape | solution.py:488
  43.6 0.6 %copy.11 = f32[1,1,16,256]{3,2,1,0:T(8,128)} copy(f32[1,1,16,256]{3,2,1,0:T(8,128)S(1)} %bitcast.1) | data formatting | bytes 32768
  44.2 1.3 %copy.12 = bf16[256,32,128]{2,1,0:T(8,128)(2,1)} copy(bf16[256,32,128]{2,1,0:T(8,128)(2,1)S(1)} %get-tuple-element.14) | data formatting | bytes 4194304

commit v3 on v2

--- a/solution.py
+++ b/solution.py
@@ -130,7 +130,8 @@
         send_halo(k)
         return carry
 
-    lax.fori_loop(1, nk, pack_on, 0)
+    ahead = min(4, nk)
+    lax.fori_loop(1, ahead, pack_on, 0)
 
     arow, acol = iota((m, m), 0), iota((m, m), 1)
     same = lax.div(arow, rows) == lax.div(acol, rows)
@@ -233,7 +234,12 @@
     def _():
         edge(0).start()
 
-    lax.fori_loop(2, nk, both, 0)
+    def all_three(k, carry):
+        pack_on(k + ahead - 2, carry)
+        return both(k, carry)
+
+    lax.fori_loop(2, nk - ahead + 2, all_three, 0)
+    lax.fori_loop(nk - ahead + 2, nk, both, 0)
 
     @pl.when(c < n_chan - 1)
     def _():

time: 45.7 us -> 44.5 us (0.974)
  Pallas kernels: 42.3 us -> 41.1 us
    pallas_call x1, Pallas kernels: 42.3 us -> 41.1 us  [step(): pl.pallas_call(functools.partial(kernel, n_chan, n_tile, send_count), out...]
where the time goes in v3:
time: 44.5 us; the launch traced here: 44.3 us
  Pallas kernels  41.1 us (92%)
  local copies, waits for them, and re-layouts  2.59 us (6%)
  between operations  0.64 us (1%)
    pallas_call x1, Pallas kernels, step(): pl.pallas_call(functools.partial(kernel, n_chan, n_tile, send_count), out...  41.1 us
    unnamed x2, local copies, waits for them, and re-layouts  1.92 us

profile of v3, /device:TPU:0, one launch (start us, length us, event | category | flops | bytes accessed | tf_op | source)
XLA Modules:
  0.0 44.3 jit_solution(12745136263290047933)
XLA Ops:
  0.6 41.1 %shard_map.85 = (f32[8,16,128]{2,1,0:T(8,128)S(1)}, f32[16,256]{1,0:T(8,128)S(1)}, bf16[256,32,128]{2,1,0:T(8,128)(2,1)S(1)}) custom-call(bf16[64,32,512]{2,1,0:T(8,128)(2,1)} %x_hbm.1, s32[1,1,4]{2,1,0:T(1,128)} %pick_hbm.1, s32[1,1,4]{2,1,0:T(1,128)} %owner_hbm.1, s32[1,1,4]{2,1,0:T(1,128)} %source_hbm.1, s32[1,1,4,1024]{3,2,1,0:T(4,128)} %low_hbm.1, ...), custom_call_target="tpu_custom_call" | custom-call | tf_op jit(solution)/shard_map/pallas_call | solution.py:453
  41.7 0.7 %reshape.12 = f32[1,1,8,2,1024]{4,3,2,1,0:T(2,128)} reshape(f32[8,16,128]{2,1,0:T(8,128)S(1)} %get-tuple-element.6) | data formatting | bytes 131072 | tf_op jit(solution)/shard_map/reshape | solution.py:494
  42.4 0.6 %copy.11 = f32[1,1,16,256]{3,2,1,0:T(8,128)} copy(f32[1,1,16,256]{3,2,1,0:T(8,128)S(1)} %bitcast.1) | data formatting | bytes 32768
  43.0 1.3 %copy.12 = bf16[256,32,128]{2,1,0:T(8,128)(2,1)} copy(bf16[256,32,128]{2,1,0:T(8,128)(2,1)S(1)} %get-tuple-element.14) | data formatting | bytes 4194304

commit v4 on v3

--- a/solution.py
+++ b/solution.py
@@ -130,7 +130,7 @@
         send_halo(k)
         return carry
 
-    ahead = min(4, nk)
+    ahead = min(3, nk)
     lax.fori_loop(1, ahead, pack_on, 0)
 
     arow, acol = iota((m, m), 0), iota((m, m), 1)
@@ -215,7 +215,7 @@
             return carry
 
         lax.fori_loop(0, KC, one, 0, unroll=2)
-        for slot, p in enumerate(peers):
+        for slot, p in enumerate(peers[:-1]):
             data(slot, c, p, k).start()
         out_ref[pl.ds(c * nch + k * KC, KC)] = stage[c, pl.ds(k * KC, KC)]
 
@@ -258,6 +258,12 @@
         return carry
 
     lax.fori_loop(0, 2, last, 0)
+
+    def beside(k, carry):
+        data(len(peers) - 1, c, peers[-1], k).start()
+        return carry
+
+    lax.fori_loop(0, nk, beside, 0)
 
     for copy in small:
         copy.wait()

time: 44.5 us -> 43.5 us (0.978)
  Pallas kernels: 41.1 us -> 40.1 us
    pallas_call x1, Pallas kernels: 41.1 us -> 40.1 us  [step(): pl.pallas_call(functools.partial(kernel, n_chan, n_tile, send_count), out...]
where the time goes in v4:
time: 43.5 us; the launch traced here: 43.3 us
  Pallas kernels  40.1 us (92%)
  local copies, waits for them, and re-layouts  2.59 us (6%)
  between operations  0.64 us (1%)
    pallas_call x1, Pallas kernels, step(): pl.pallas_call(functools.partial(kernel, n_chan, n_tile, send_count), out...  40.1 us
    unnamed x2, local copies, waits for them, and re-layouts  1.92 us

profile of v4, /device:TPU:0, one launch (start us, length us, event | category | flops | bytes accessed | tf_op | source)
XLA Modules:
  0.0 43.3 jit_solution(10859465952853749327)
XLA Ops:
  0.6 40.1 %shard_map.85 = (f32[8,16,128]{2,1,0:T(8,128)S(1)}, f32[16,256]{1,0:T(8,128)S(1)}, bf16[256,32,128]{2,1,0:T(8,128)(2,1)S(1)}) custom-call(bf16[64,32,512]{2,1,0:T(8,128)(2,1)} %x_hbm.1, s32[1,1,4]{2,1,0:T(1,128)} %pick_hbm.1, s32[1,1,4]{2,1,0:T(1,128)} %owner_hbm.1, s32[1,1,4]{2,1,0:T(1,128)} %source_hbm.1, s32[1,1,4,1024]{3,2,1,0:T(4,128)} %low_hbm.1, ...), custom_call_target="tpu_custom_call" | custom-call | tf_op jit(solution)/shard_map/pallas_call | solution.py:459
  40.7 0.7 %reshape.12 = f32[1,1,8,2,1024]{4,3,2,1,0:T(2,128)} reshape(f32[8,16,128]{2,1,0:T(8,128)S(1)} %get-tuple-element.6) | data formatting | bytes 131072 | tf_op jit(solution)/shard_map/reshape | solution.py:500
  41.4 0.6 %copy.11 = f32[1,1,16,256]{3,2,1,0:T(8,128)} copy(f32[1,1,16,256]{3,2,1,0:T(8,128)S(1)} %bitcast.1) | data formatting | bytes 32768
  42.0 1.3 %copy.12 = bf16[256,32,128]{2,1,0:T(8,128)(2,1)} copy(bf16[256,32,128]{2,1,0:T(8,128)(2,1)S(1)} %get-tuple-element.14) | data formatting | bytes 4194304
